TPU v7x, 32 devices: a whole 2x2x4 slice. The times are simulated.
32 devices in a mesh: groups: 2 (over y), node: 4 (over z), tensor: 2 (over x), pair: 2 (over core).
Axes of the slice: x: 2, y: 2, z: 4, core: 2. Of those that a mesh axis runs over, the one named last changes fastest.
Arguments:
- attention_partial: bfloat16 [4, 128, 6144], P(('tensor', 'pair'), ('groups', 'node')), parts along dimension 1, may hold values from -4 to 4
- residual: bfloat16 [8, 4, 4, 6144], P(('groups', 'node'), ('tensor', 'pair')), parts along dimension 0, may hold values from -6 to 6
- norm_scale: bfloat16 [6144], replicated, may hold values from 0.099609375 to 1.8984375
- router_matrix: bfloat16 [6144, 4], replicated, may hold values from -0.078125 to 0.078125
- up_matrix: bfloat16 [4, 6144, 8192], P('node', None, ('tensor', 'pair')), may hold values from -0.078125 to 0.078125
- down_matrix: bfloat16 [4, 8192, 6144], P('node', None, ('tensor', 'pair')), may hold values from -0.0625 to 0.0625
- adapter_in_maps: bfloat16 [4, 4, 6144, 16], P(None, None, ('tensor', 'pair')), may hold values from -0.078125 to 0.078125
- adapter_out_maps: bfloat16 [4, 4, 16, 8192], P(None, 'node', None, ('tensor', 'pair')), may hold values from -1.5 to 1.5
- token_experts: int32 [8, 4, 4, 2], P(('groups', 'node'), ('tensor', 'pair')), parts along dimension 0, may hold values from 0 to 3, as said below
- token_requests: int32 [8, 4, 4], P(('groups', 'node'), ('tensor', 'pair')), parts along dimension 0, may hold values from 0 to 7, as said below
- request_adapters: int32 [16], P('groups'), parts along dimension 0, may hold values from 0 to 3
Outputs:
- mixed: bfloat16 [8, 4, 4, 6144], P(('groups', 'node'), ('tensor', 'pair')), parts along dimension 0
There are 2 independent parts, one for each index of `groups`. A program takes and returns all parts, laid end to end along the dimension named above; an argument that names none is the same for every part. Nothing has to cross between parts.
Inputs may be any that keep to these rules, and one draw needn't show every extreme that they name: `token_experts`: each token names two different experts. In every aligned block of 4 tokens (the tokens of one device), the experts are named by 3, 2, 2 and 1 tokens in some order. `token_requests`: never falling along the tokens; every request has one or more tokens.
All inputs are finite; a program needn't handle non-finite values.
Results may differ from a plain program's by a relative error of at most 0.013.
Values may be sent and summed in bfloat16 or wider, within the bound.
A program may use at most 128 MiB of HBM per device.

v0:
```python
import jax
import jax.numpy as jnp
from jax import lax
from jax.sharding import PartitionSpec as P

EXPERT_COUNT = 4
ADAPTER_RANK = 16
ADAPTER_COUNT = 4
CAP = 3


def silu_value(value):
    return value / (1.0 + jnp.exp(-value))


def slot_table(routes):
    flat_routes = routes.reshape(-1)
    same = flat_routes[:, None] == flat_routes[None, :]
    order = jnp.arange(flat_routes.shape[0])
    earlier = order[None, :] < order[:, None]
    return jnp.sum((same & earlier).astype(jnp.int32), axis=1).reshape(routes.shape)


def route_hits(routes, node_count, share):
    slots = slot_table(routes)
    node_expert = jnp.arange(node_count) // share
    slot_index = jnp.arange(CAP)
    return (routes[None, None, :, :] == node_expert[:, None, None, None]) & (
        slots[None, None, :, :] == slot_index[None, :, None, None]
    )


def on_device(
    attention_partial,
    residual,
    norm_scale,
    router_matrix,
    up_matrix,
    down_matrix,
    adapter_in_maps,
    adapter_out_maps,
    token_experts,
    token_requests,
    request_adapters,
):
    node_count = lax.axis_size("node")
    chip_groups = lax.axis_size("tensor") * lax.axis_size("pair")
    share = node_count // EXPERT_COUNT
    own_count = residual.shape[2]
    partial_rows = attention_partial[0].astype(jnp.float32)
    summed = lax.psum(partial_rows.astype(jnp.bfloat16), ("tensor", "pair")).astype(jnp.float32)
    own_rows = lax.dynamic_slice_in_dim(
        summed, lax.axis_index(("tensor", "pair")) * own_count, own_count, 0
    )
    head_total = residual[0, 0].astype(jnp.float32) + own_rows
    mean_square = jnp.mean(head_total * head_total, axis=1, keepdims=True)
    normalized_input = (
        head_total * lax.rsqrt(mean_square + 1e-05) * norm_scale.astype(jnp.float32)
    ).astype(jnp.bfloat16)
    logits = jnp.dot(normalized_input, router_matrix, preferred_element_type=jnp.float32)
    routes = token_experts[0, 0]
    chosen = jnp.take_along_axis(logits, routes, axis=1)
    first_gate = 1.0 / (1.0 + jnp.exp(chosen[:, 1] - chosen[:, 0]))
    gates = jnp.stack([first_gate, 1.0 - first_gate], axis=1)
    request_pick = token_requests[0, 0][:, None] == jnp.arange(request_adapters.shape[0])[None, :]
    adapters = jnp.sum(request_pick.astype(jnp.int32) * request_adapters[None, :], axis=1)
    route_hit = route_hits(routes, node_count, share)
    table = jnp.any(route_hit, axis=3)
    combine_weight = jnp.sum(route_hit.astype(jnp.float32) * gates[None, None, :, :], axis=3)
    send = jnp.einsum(
        "jsk,kd->jsd",
        table.astype(jnp.bfloat16),
        normalized_input,
        preferred_element_type=jnp.float32,
    ).astype(jnp.bfloat16)
    send_ids = jnp.sum(table.astype(jnp.int32) * adapters[None, None, :], axis=2)
    arrived, arrived_ids = (
        lax.all_to_all(send, "node", split_axis=0, concat_axis=0, tiled=True),
        lax.all_to_all(send_ids, "node", split_axis=0, concat_axis=0, tiled=True),
    )
    gathered, gathered_ids = (
        lax.all_gather(arrived[None], ("tensor", "pair"), axis=0, tiled=True),
        lax.all_gather(arrived_ids[None], ("tensor", "pair"), axis=0, tiled=True),
    )
    model_width = normalized_input.shape[1]
    flat_rows = gathered.reshape(-1, model_width)
    flat_ids = gathered_ids.reshape(-1)
    row_count = flat_rows.shape[0]
    col_width = model_width // chip_groups
    expert_index = lax.axis_index("node") // share
    part_index = lax.axis_index(("tensor", "pair"))
    slice_rows = lax.dynamic_slice_in_dim(flat_rows, part_index * col_width, col_width, 1)
    adapter_input = lax.dynamic_index_in_dim(adapter_in_maps, expert_index, 1, keepdims=False)
    in_columns = jnp.transpose(adapter_input, (1, 0, 2)).reshape(
        col_width, ADAPTER_COUNT * ADAPTER_RANK
    )
    adapter_choice = flat_ids[:, None] == jnp.arange(ADAPTER_COUNT)[None, :]
    projected = jnp.dot(slice_rows, in_columns, preferred_element_type=jnp.float32).reshape(
        row_count, ADAPTER_COUNT, ADAPTER_RANK
    )
    middle_part = jnp.sum(projected * adapter_choice[:, :, None].astype(jnp.float32), axis=1)
    adapter_middle = lax.psum(middle_part.astype(jnp.bfloat16), ("tensor", "pair"))
    spread_rows = (
        adapter_middle[:, None, :] * adapter_choice[:, :, None].astype(jnp.bfloat16)
    ).reshape(row_count, ADAPTER_COUNT * ADAPTER_RANK)
    output_columns = adapter_out_maps[:, 0].reshape(
        ADAPTER_COUNT * ADAPTER_RANK, adapter_out_maps.shape[3]
    )
    up_projection = jnp.dot(flat_rows, up_matrix[0], preferred_element_type=jnp.float32)
    up_projection = up_projection + jnp.dot(
        spread_rows, output_columns, preferred_element_type=jnp.float32
    )
    hidden = silu_value(up_projection).astype(jnp.bfloat16)
    down_local = down_matrix[0]
    down_value = jnp.dot(
        lax.all_gather(hidden, ("tensor", "pair"), axis=1, tiled=True),
        down_local,
        preferred_element_type=jnp.float32,
    ).astype(jnp.bfloat16)
    arranged = down_value.reshape(chip_groups, node_count, CAP, col_width)
    returned = lax.all_to_all(
        lax.all_to_all(arranged, "node", split_axis=1, concat_axis=1, tiled=True),
        ("tensor", "pair"),
        split_axis=0,
        concat_axis=3,
        tiled=True,
    )
    contrib = returned.reshape(node_count, CAP, model_width).astype(jnp.float32)
    moe_total = jnp.einsum("jsk,jsd->kd", combine_weight, contrib, precision=lax.Precision.HIGHEST)
    mixed = (head_total + moe_total).astype(jnp.bfloat16)
    return mixed.reshape(1, 1, own_count, model_width)


def solution(mesh):
    in_specs = (
        P(("tensor", "pair"), ("groups", "node"), None),
        P(("groups", "node"), ("tensor", "pair"), None, None),
        P(),
        P(),
        P("node", None, ("tensor", "pair")),
        P("node", None, ("tensor", "pair")),
        P(None, None, ("tensor", "pair"), None),
        P(None, "node", None, ("tensor", "pair")),
        P(("groups", "node"), ("tensor", "pair"), None, None),
        P(("groups", "node"), ("tensor", "pair"), None),
        P("groups"),
    )
    out_specs = P(("groups", "node"), ("tensor", "pair"), None, None)
    return jax.shard_map(
        on_device, mesh=mesh, in_specs=in_specs, out_specs=out_specs, check_vma=False
    )
```

profile of v0, /device:TPU:0, one launch (start us, length us, event | category | flops | bytes accessed | tf_op | source)
XLA Modules:
  0.0 133.3 jit_solution(4548190264912166332)
XLA Ops:
  6.5 0.7 all-reduce.2.cloned.1.call-update
  7.3 0.8 copy.37
  8.0 0.1 eq.96
  8.1 0.2 convert_reduce_fusion
  8.3 0.1 eq.100
  8.4 0.1 copy.38
  8.5 0.7 iota_compare_fusion.1
  9.2 0.9 select_reduce_fusion.1
  10.1 0.2 select_reduce_fusion
  10.2 0.7 copy.43
  10.9 6.3 %all-to-all-start.1 = ((s32[4,1,3]{2,1,0:T(1,128)}), s32[4,1,3]{2,1,0:T(1,128)S(1)}, u32[]{:S(2)}, u32[]{:S(2)}) async-start(s32[4,1,3]{2,1,0:T(1,128)} %copy.43), calls=%async_computation.1 | async-start | bytes 4096 | tf_op jit(solution)/shard_map/all_to_all | solution.py:79
  17.2 0.7 fusion.22
  17.9 0.7 convert_element_type.60
  18.6 0.1 copy.39
  18.7 0.1 reshape.160
  18.8 3.9 %all-to-all-done.1 = s32[4,1,3]{2,1,0:T(1,128)S(1)} async-done(((s32[4,1,3]{2,1,0:T(1,128)}), s32[4,1,3]{2,1,0:T(1,128)S(1)}, u32[]{:S(2)}, u32[]{:S(2)}) %all-to-all-start.1) | async-done | bytes 80 | tf_op jit(solution)/shard_map/all_to_all | solution.py:79
  22.7 5.1 %all-gather.1 = s32[16,1,3]{2,1,0:T(1,128)S(1)} all-gather(s32[4,1,3]{2,1,0:T(1,128)S(1)} %all-to-all-done.1), channel_id=3, replica_groups=mesh['groups'=2,'node'=4,'tensor'=2,'pair'=2] {'tensor','pair'}, dimensions={0}, use_global_device_ids=true | all-gather | bytes 240 | tf_op jit(solution)/shard_map/all_gather | solution.py:83
  27.8 0.5 broadcast.173
  28.3 0.7 reduce.3
  29.0 0.1 eq.108
  29.1 15.0 %all-reduce.2.cloned.1.call-done = bf16[16,6144]{1,0:T(8,128)(2,1)} async-done(((bf16[16,6144]{1,0:T(8,128)(2,1)}), bf16[16,6144]{1,0:T(8,128)(2,1)}) %all-reduce.2.cloned.1.call-update) | async-done | bytes 196624 | tf_op jit(solution)/shard_map/psum | solution.py:51
  44.1 1.1 multiply_reduce_fusion
  45.2 1.0 multiply_convert_fusion
  46.2 0.2 convolution_convert_fusion
  46.4 1.0 fusion.24
  47.4 0.7 gather_fusion
  48.1 0.1 copy.40
  48.2 0.8 copy.41
  49.1 4.6 %all-to-all-start = ((bf16[4,3,6144]{2,1,0:T(4,128)(2,1)}), bf16[4,3,6144]{2,1,0:T(4,128)(2,1)S(1)}, u32[]{:S(2)}, u32[]{:S(2)}) async-start(bf16[4,3,6144]{2,1,0:T(4,128)(2,1)} %copy.41), calls=%async_computation | async-start | bytes 393216 | tf_op jit(solution)/shard_map/all_to_all | solution.py:78
  53.7 0.7 and_select_fusion.1
  54.3 5.6 %all-to-all-done = bf16[4,3,6144]{2,1,0:T(4,128)(2,1)S(1)} async-done(((bf16[4,3,6144]{2,1,0:T(4,128)(2,1)}), bf16[4,3,6144]{2,1,0:T(4,128)(2,1)S(1)}, u32[]{:S(2)}, u32[]{:S(2)}) %all-to-all-start) | async-done | bytes 147488 | tf_op jit(solution)/shard_map/all_to_all | solution.py:78
  59.9 7.9 %all-gather = bf16[16,3,6144]{2,1,0:T(4,128)(2,1)S(1)} all-gather(bf16[4,3,6144]{2,1,0:T(4,128)(2,1)S(1)} %all-to-all-done), channel_id=2, replica_groups=mesh['groups'=2,'node'=4,'tensor'=2,'pair'=2] {'tensor','pair'}, dimensions={0}, use_global_device_ids=true | all-gather | bytes 737280 | tf_op jit(solution)/shard_map/all_gather | solution.py:82
  67.8 0.5 reshape.154
  68.3 10.5 %fusion.2 = f32[48,2048]{1,0:T(8,128)S(1)} fusion(bf16[48,6144]{1,0:T(8,128)(2,1)S(1)} %reshape.154, bf16[1,6144,2048]{2,1,0:T(8,128)(2,1)} %param.15), kind=kOutput, calls=%fused_computation.3 | convolution fusion | flops 1207959552 | bytes 26148864 | tf_op jit(solution)/shard_map/dot_general | solution.py:109
  78.8 0.2 fusion.10
  79.0 6.8 %psum.15 = bf16[48,16]{0,1:T(8,128)(2,1)S(1)} all-reduce(bf16[48,16]{0,1:T(8,128)(2,1)S(1)} %fusion.10), channel_id=1, replica_groups=mesh['groups'=2,'node'=4,'tensor'=2,'pair'=2] {'tensor','pair'}, use_global_device_ids=true, to_apply=%region_8.9 | all-reduce | flops 768 | bytes 3072 | tf_op jit(solution)/shard_map/psum | solution.py:102
  85.9 0.3 divide_convert_fusion
  86.2 7.9 %all_gather.11 = bf16[48,8192]{1,0:T(8,128)(2,1)S(1)} all-gather(bf16[48,2048]{1,0:T(8,128)(2,1)S(1)} %divide_convert_fusion), channel_id=1, replica_groups=mesh['groups'=2,'node'=4,'tensor'=2,'pair'=2] {'tensor','pair'}, dimensions={1}, use_global_device_ids=true | all-gather | bytes 983040 | tf_op jit(solution)/shard_map/all_gather | solution.py:116
  94.1 10.4 %fusion.7 = bf16[48,1536]{1,0:T(8,128)(2,1)S(1)} fusion(bf16[48,8192]{1,0:T(8,128)(2,1)S(1)} %all_gather.11, bf16[1,8192,1536]{2,1,0:T(8,128)(2,1)} %param.16), kind=kOutput, calls=%fused_computation.11 | convolution fusion | flops 1208033280 | bytes 26099712 | tf_op jit(solution)/shard_map/dot_general | solution.py:115
  104.5 0.1 reshape.156
  104.6 0.8 copy.44
  105.4 3.3 %all-to-all-start.2 = ((bf16[4,4,3,1536]{3,0,2,1:T(4,128)(2,1)}), bf16[4,4,3,1536]{3,0,2,1:T(4,128)(2,1)S(1)}, u32[]{:S(2)}, u32[]{:S(2)}) async-start(bf16[4,4,3,1536]{3,0,2,1:T(4,128)(2,1)} %copy.44), calls=%async_computation.2 | async-start | bytes 294912 | tf_op jit(solution)/shard_map/all_to_all | solution.py:122
  108.8 6.7 %all-to-all-done.2 = bf16[4,4,3,1536]{3,0,2,1:T(4,128)(2,1)S(1)} async-done(((bf16[4,4,3,1536]{3,0,2,1:T(4,128)(2,1)}), bf16[4,4,3,1536]{3,0,2,1:T(4,128)(2,1)S(1)}, u32[]{:S(2)}, u32[]{:S(2)}) %all-to-all-start.2) | async-done | bytes 147488 | tf_op jit(solution)/shard_map/all_to_all | solution.py:122
  115.6 0.7 copy.45
  116.3 3.3 %all-to-all-start.3 = ((bf16[4,4,3,1536]{3,1,2,0:T(4,128)(2,1)}), bf16[4,4,3,1536]{3,1,2,0:T(4,128)(2,1)S(1)}, u32[]{:S(2)}, u32[]{:S(2)}) async-start(bf16[4,4,3,1536]{3,1,2,0:T(4,128)(2,1)} %copy.45), calls=%async_computation.3 | async-start | bytes 294912 | tf_op jit(solution)/shard_map/all_to_all | solution.py:121
  119.6 4.8 %all-to-all-done.3 = bf16[4,4,3,1536]{3,1,2,0:T(4,128)(2,1)S(1)} async-done(((bf16[4,4,3,1536]{3,1,2,0:T(4,128)(2,1)}), bf16[4,4,3,1536]{3,1,2,0:T(4,128)(2,1)S(1)}, u32[]{:S(2)}, u32[]{:S(2)}) %all-to-all-start.3) | async-done | bytes 147488 | tf_op jit(solution)/shard_map/all_to_all | solution.py:121
  124.4 0.1 reshape.157
  124.6 1.9 %fusion.6 = bf16[1,1,4,6144]{3,2,1,0:T(4,128)(2,1)} fusion(f32[4,3,4]{2,0,1:T(4,128)S(1)} %fusion.16, bf16[4,3,6144]{2,0,1:T(4,128)(2,1)S(1)} %reshape.157, bf16[1,1,4,6144]{3,2,1,0:T(4,128)(2,1)S(1)} %copy-done.1, bf16[16,6144]{1,0:T(8,128)(2,1)} %all-reduce.2.cloned.1.call-done, s32[]{:T(128)S(6)} %select_n.36), kind=kOutput, calls=%fused_computation.9 | convolution fusion | flops 3661824 | bytes 295108 | tf_op jit(solution)/shard_map/jsk,jsd->kd/dot_general | solution.py:129
  (17 shorter events, 0.2 us)
Async XLA Ops:
  6.5 72.3 %copy-start = (bf16[4,4,1536,16]{2,3,1,0:T(8,128)(2,1)S(1)}, bf16[4,4,1536,16]{2,3,1,0:T(8,128)(2,1)}, u32[]{:S(2)}) copy-start(bf16[4,4,1536,16]{2,3,1,0:T(8,128)(2,1)} %param.17) | copy-start | bytes 2359300
  6.5 79.4 %copy-start.2 = (bf16[4,1,16,2048]{3,2,1,0:T(8,128)(2,1)S(1)}, bf16[4,1,16,2048]{3,2,1,0:T(8,128)(2,1)}, u32[]{:S(2)}) copy-start(bf16[4,1,16,2048]{3,2,1,0:T(8,128)(2,1)} %param.18) | copy-start | bytes 786436
  6.5 37.6 %all-reduce.2.cloned.1.call-start = ((), (), s32[]{:S(2)}) async-start(), calls=%async_computation.4 | async-start | bytes 393216 | tf_op jit(solution)/shard_map/psum | solution.py:51
  10.9 11.8 %all-to-all-start.1 = ((s32[4,1,3]{2,1,0:T(1,128)}), s32[4,1,3]{2,1,0:T(1,128)S(1)}, u32[]{:S(2)}, u32[]{:S(2)}) async-start(s32[4,1,3]{2,1,0:T(1,128)} %copy.43), calls=%async_computation.1 | async-start | bytes 4096 | tf_op jit(solution)/shard_map/all_to_all | solution.py:79
  49.1 10.9 %all-to-all-start = ((bf16[4,3,6144]{2,1,0:T(4,128)(2,1)}), bf16[4,3,6144]{2,1,0:T(4,128)(2,1)S(1)}, u32[]{:S(2)}, u32[]{:S(2)}) async-start(bf16[4,3,6144]{2,1,0:T(4,128)(2,1)} %copy.41), calls=%async_computation | async-start | bytes 393216 | tf_op jit(solution)/shard_map/all_to_all | solution.py:78
  78.8 45.7 %copy-start.1 = (bf16[1,1,4,6144]{3,2,1,0:T(4,128)(2,1)S(1)}, bf16[1,1,4,6144]{3,2,1,0:T(4,128)(2,1)}, u32[]{:S(2)}) copy-start(bf16[1,1,4,6144]{3,2,1,0:T(4,128)(2,1)} %param.12) | copy-start | bytes 147460
  105.4 10.1 %all-to-all-start.2 = ((bf16[4,4,3,1536]{3,0,2,1:T(4,128)(2,1)}), bf16[4,4,3,1536]{3,0,2,1:T(4,128)(2,1)S(1)}, u32[]{:S(2)}, u32[]{:S(2)}) async-start(bf16[4,4,3,1536]{3,0,2,1:T(4,128)(2,1)} %copy.44), calls=%async_computation.2 | async-start | bytes 294912 | tf_op jit(solution)/shard_map/all_to_all | solution.py:122
  116.3 8.1 %all-to-all-start.3 = ((bf16[4,4,3,1536]{3,1,2,0:T(4,128)(2,1)}), bf16[4,4,3,1536]{3,1,2,0:T(4,128)(2,1)S(1)}, u32[]{:S(2)}, u32[]{:S(2)}) async-start(bf16[4,4,3,1536]{3,1,2,0:T(4,128)(2,1)} %copy.45), calls=%async_computation.3 | async-start | bytes 294912 | tf_op jit(solution)/shard_map/all_to_all | solution.py:121
Sparse Core Ops, SparseCore 0:
  9.7 34.3 all-reduce.1
where the time goes:
time: 134 us; the launch traced here: 133 us
  waiting for transfers between devices  36.7 us (27%)
  blocking collectives  27.8 us (21%)
  matrix products  24.4 us (18%)
  starting transfers between devices  17.6 us (13%)
  between operations  13.6 us (10%)
  other arithmetic  6.83 us (5%)
  local copies, waits for them, and re-layouts  6.43 us (5%)
    psum x1, waiting for transfers between devices, on_device(): lax.psum(partial_rows.astype(jnp.bfloat16), ('tensor', 'pair'))  15 us
    dot_general x1, matrix products, on_device(): jnp.dot(flat_rows, up_matrix[0], preferred_element_type=jnp.float32)  10.5 us
    dot_general x1, matrix products, on_device(): jnp.dot(lax.all_gather(hidden, ('tensor', 'pair'), axis=1, tiled=True), d...  10.4 us
    all_gather x1, blocking collectives, on_device(): lax.all_gather(hidden, ('tensor', 'pair'), axis=1, tiled=True)  7.91 us
    all_gather x1, blocking collectives, on_device(): lax.all_gather(arrived[None], ('tensor', 'pair'), axis=0, tiled=True)  7.9 us
    psum x1, blocking collectives, on_device(): lax.psum(middle_part.astype(jnp.bfloat16), ('tensor', 'pair'))  6.84 us
    all_to_all x1, waiting for transfers between devices, on_device(): lax.all_to_all(arranged, 'node', split_axis=1, concat_axis=1, tiled=True)  6.75 us
    all_to_all x1, starting transfers between devices, on_device(): lax.all_to_all(send_ids, 'node', split_axis=0, concat_axis=0, tiled=True)  6.32 us
  transfers between devices with their start and end apart: 5, of which 5 were waited for; matrix products, arithmetic and copies ran while one was open for 5% of the time, Pallas kernels for 0%

commit v1 on v0

v1 whole, which is shorter than its diff:
```python
import functools

import jax
import jax.numpy as jnp
from jax import lax
from jax.experimental import pallas as pl
from jax.experimental.pallas import tpu as pltpu
from jax.sharding import PartitionSpec as P

EXPERT_COUNT = 4
MESH = pl.DeviceIdType.MESH
F32 = jnp.float32
BF16 = jnp.bfloat16


def kernel(
    dims,
    ap_ref,
    res_ref,
    scale_ref,
    router_ref,
    up_ref,
    down_ref,
    in_ref,
    outmap_ref,
    te_ref,
    tr_ref,
    ra_ref,
    out_ref,
    w_up,
    w_down,
    a_in,
    ap_buf,
    res_buf,
    head,
    y_buf,
    inf_buf,
    inf_all,
    part_buf,
    meta,
    lora_buf,
    acc,
    hid,
    acc_down,
    piece,
    ret,
    outb,
    up_sem,
    down_sem,
    loc_sem,
    ap_s,
    ap_r,
    res_s,
    res_r,
    inf_s,
    inf_r,
    part_s,
    part_r,
    meta_s,
    meta_r,
    z_s,
    z_r,
    x_s,
    x_r,
    p_s,
    p_r,
    lora_s,
    lora_r,
    hx_s,
    hx_r,
    hp_s,
    hp_r,
    ret_s,
    ret_r,
    out_s,
    out_r,
):
    nodes, tensors, groups, own, block, cols, width, chunks, chunk, rank, adapters, share = dims
    z = lax.axis_index("node")
    t = lax.axis_index("tensor")
    p = lax.axis_index("pair")
    c = t * 2 + p
    q = 1 - p
    tokens = nodes * block

    def at_cols(index):
        return pl.ds(pl.multiple_of(index * cols, cols), cols)

    def at_block(index):
        return pl.ds(pl.multiple_of(index * block, block), block)

    def to_chip(index):
        return {"tensor": index // 2, "pair": lax.rem(index, 2)}

    def remote(src, dst, send, recv, device):
        return pltpu.make_async_remote_copy(
            src_ref=src, dst_ref=dst, send_sem=send, recv_sem=recv,
            device_id=device, device_id_type=MESH,
        )

    chip_to = [lax.rem(c + d, groups) for d in range(1, groups)]
    chip_from = [lax.rem(c - d + groups, groups) for d in range(1, groups)]
    node_to = [lax.rem(z + d, nodes) for d in range(1, nodes)]
    node_from = [lax.rem(z - d + nodes, nodes) for d in range(1, nodes)]
    tens_to = [lax.rem(t + d, tensors) for d in range(1, tensors)]
    tens_from = [lax.rem(t - d + tensors, tensors) for d in range(1, tensors)]
    sends = []

    def go(copy):
        copy.start()
        sends.append(copy)

    def up_copy(index):
        rows = at_cols(index)
        return pltpu.make_async_copy(up_ref.at[rows], w_up.at[rows], up_sem.at[index])

    def down_copy(index):
        rows = pl.ds(pl.multiple_of(index * width, width), width)
        return pltpu.make_async_copy(down_ref.at[rows], w_down.at[rows], down_sem.at[index])

    order = [c, t * 2 + q]
    for t2 in tens_from:
        order.append(t2 * 2 + p)
    for t2 in tens_from:
        order.append(t2 * 2 + q)

    own_ap = pltpu.make_async_copy(ap_ref.at[:, at_cols(c)], ap_buf.at[c], loc_sem.at[0])
    own_ap.start()
    in_copy = pltpu.make_async_copy(in_ref.at[:, z // share], a_in, loc_sem.at[1])
    in_copy.start()
    for index in order:
        up_copy(index).start()

    barrier = pltpu.get_barrier_semaphore()
    for c2 in chip_to:
        pl.semaphore_signal(barrier, inc=1, device_id=to_chip(c2), device_id_type=MESH)
    for z2 in node_to:
        pl.semaphore_signal(barrier, inc=1, device_id={"node": z2}, device_id_type=MESH)

    row8 = lax.broadcasted_iota(jnp.int32, (8, 128), 0)
    lane8 = lax.broadcasted_iota(jnp.int32, (8, 128), 1)
    info = jnp.zeros((8, 128), jnp.int32)
    for k in range(own):
        here = row8 == k
        info = jnp.where(here & (lane8 == 0), ra_ref[tr_ref[k]], info)
        info = jnp.where(here & (lane8 == 1), te_ref[k, 0], info)
        info = jnp.where(here & (lane8 == 2), te_ref[k, 1], info)
    inf_buf[c] = info

    pl.semaphore_wait(barrier, groups - 1 + nodes - 1)

    for c2 in chip_to:
        go(remote(ap_ref.at[:, at_cols(c2)], ap_buf.at[c], ap_s.at[c2], ap_r.at[c], to_chip(c2)))
    for c2 in chip_to:
        go(remote(res_ref.at[:, at_cols(c2)], res_buf.at[c], res_s.at[c2], res_r.at[c], to_chip(c2)))
    for c2 in chip_to:
        go(remote(inf_buf.at[c], inf_buf.at[c], inf_s.at[c2], inf_r.at[c], to_chip(c2)))

    res_buf[c] = res_ref[:, at_cols(c)]
    for c2 in chip_from:
        remote(res_buf.at[c2], res_buf.at[c2], res_s.at[c2], res_r.at[c2], to_chip(c2)).wait_recv()
    for index in range(groups):
        head[index * own : (index + 1) * own, :] = res_buf[index].astype(F32)
    own_ap.wait()
    for c2 in chip_from:
        remote(ap_buf.at[c2], ap_buf.at[c2], ap_s.at[c2], ap_r.at[c2], to_chip(c2)).wait_recv()
    total = ap_buf[0].astype(F32)
    for index in range(1, groups):
        total = total + ap_buf[index].astype(F32)
    total = total + head[...]
    head[...] = total
    scale = scale_ref[:, at_cols(c)].astype(F32)
    y = (total * scale).astype(BF16)
    y_buf[c, at_block(z), :] = y

    def z_copy(z2, who):
        piece_ref = y_buf.at[c, at_block(who)]
        return remote(piece_ref, piece_ref, z_s.at[z2], z_r.at[who], {"node": z2})

    def x_copy(t2, who_t, zb):
        piece_ref = y_buf.at[who_t * 2 + p, at_block(zb)]
        return remote(piece_ref, piece_ref, x_s.at[t2, zb], x_r.at[who_t, zb], {"tensor": t2})

    def p_copy(t2, core, zb):
        piece_ref = y_buf.at[t2 * 2 + core, at_block(zb)]
        return remote(piece_ref, piece_ref, p_s.at[t2, zb], p_r.at[t2, zb], {"pair": q})

    def spread(zb):
        for t2 in tens_to:
            go(x_copy(t2, t, zb))
        go(p_copy(t, p, zb))

    for z2 in node_to:
        go(z_copy(z2, z))
    spread(z)

    lane = lax.broadcasted_iota(jnp.int32, (block, 128), 1)
    y32 = y.astype(F32)
    router = router_ref[:, at_cols(c)].astype(F32)
    partial = jnp.where(lane == 0, jnp.sum(total * total, axis=1, keepdims=True), 0.0)
    for e in range(EXPERT_COUNT):
        value = jnp.sum(y32 * router[e : e + 1, :], axis=1, keepdims=True)
        partial = jnp.where(lane == 1 + e, value, partial)
    part_buf[c] = partial
    for c2 in chip_to:
        go(remote(part_buf.at[c], part_buf.at[c], part_s.at[c2], part_r.at[c], to_chip(c2)))
    for index in order:
        down_copy(index).start()
    for c2 in chip_from:
        remote(inf_buf.at[c2], inf_buf.at[c2], inf_s.at[c2], inf_r.at[c2], to_chip(c2)).wait_recv()
    for index in range(groups):
        inf_all[index * own : (index + 1) * own, :] = inf_buf[index, 0:own, :]
    for c2 in chip_from:
        remote(part_buf.at[c2], part_buf.at[c2], part_s.at[c2], part_r.at[c2], to_chip(c2)).wait_recv()
    sums = part_buf[0]
    for index in range(1, groups):
        sums = sums + part_buf[index]
    root = lax.rsqrt(sums[:, 0:1] / (groups * cols) + 1e-05)
    routes = inf_all[...]
    meta[z] = jnp.where(
        lane == 0, root, jnp.where(lane == 1, routes[:, 0:1].astype(F32), 0.0)
    )
    for z2 in node_to:
        go(remote(meta.at[z], meta.at[z], meta_s.at[z2], meta_r.at[z], {"node": z2}))
    first_expert = routes[:, 1:2]
    second_expert = routes[:, 2:3]
    chosen0 = jnp.zeros((block, 1), F32)
    chosen1 = jnp.zeros((block, 1), F32)
    for e in range(EXPERT_COUNT):
        logit = sums[:, 1 + e : 2 + e] * root
        chosen0 = jnp.where(first_expert == e, logit, chosen0)
        chosen1 = jnp.where(second_expert == e, logit, chosen1)
    gate0 = 1.0 / (1.0 + jnp.exp(chosen1 - chosen0))
    gate1 = 1.0 - gate0

    for z2 in node_from:
        z_copy(z2, z2).wait_recv()
        spread(z2)

    in_copy.wait()
    wide = adapters * rank
    mid = lax.dot_general(
        y_buf[c], a_in[...].reshape(wide, cols), (((1,), (1,)), ((), ())),
        preferred_element_type=F32,
    )
    lora_buf[c] = mid.astype(BF16)
    for c2 in chip_to:
        go(remote(lora_buf.at[c], lora_buf.at[c], lora_s.at[c2], lora_r.at[c], to_chip(c2)))

    def up_part(index, j):
        lanes = pl.ds(pl.multiple_of(j * chunk, chunk), chunk)
        rows = at_cols(index)
        return jnp.dot(y_buf[index], w_up[rows, lanes], preferred_element_type=F32)

    def up_step(index, first):
        up_copy(index).wait()

        def body(j, carry):
            value = up_part(index, j)
            acc[j] = value if first else acc[j] + value
            return carry

        lax.fori_loop(0, chunks, body, 0)

    up_step(order[0], True)
    for zb in range(nodes):
        p_copy(t, q, zb).wait_recv()
    up_step(order[1], False)
    for t2 in tens_from:
        for zb in [z] + node_from:
            x_copy(t2, t2, zb).wait_recv()
            go(p_copy(t2, p, zb))
        up_step(t2 * 2 + p, False)

    for c2 in chip_from:
        remote(lora_buf.at[c2], lora_buf.at[c2], lora_s.at[c2], lora_r.at[c2], to_chip(c2)).wait_recv()
    for z2 in node_from:
        remote(meta.at[z2], meta.at[z2], meta_s.at[z2], meta_r.at[z2], {"node": z2}).wait_recv()
    facts = meta[...].reshape(tokens, 128)
    root_all = facts[:, 0:1]
    low = facts[:, 1:2] * float(rank)
    mid = lora_buf[0].astype(F32)
    for index in range(1, groups):
        mid = mid + lora_buf[index].astype(F32)
    slot = lax.broadcasted_iota(jnp.int32, (tokens, wide), 1).astype(F32)
    mid = jnp.where((slot >= low) & (slot < low + rank), mid * root_all, 0.0).astype(BF16)

    last = [t2 * 2 + q for t2 in tens_from]
    for i, t2 in enumerate(tens_from):
        for zb in range(nodes):
            p_copy(t2, q, zb).wait_recv()
        if i < len(last) - 1:
            up_step(last[i], False)

    def hx_copy(t2, who_t, j):
        piece_ref = hid.at[who_t * 2 + p, j]
        return remote(piece_ref, piece_ref, hx_s.at[t2, j], hx_r.at[who_t, j], {"tensor": t2})

    def hp_copy(t2, core, j):
        piece_ref = hid.at[t2 * 2 + core, j]
        return remote(piece_ref, piece_ref, hp_s.at[t2, j], hp_r.at[t2, j], {"pair": q})

    if last:
        up_copy(last[-1]).wait()

    def hidden_step(j, carry):
        lanes = pl.ds(pl.multiple_of(j * chunk, chunk), chunk)
        value = acc[j]
        if last:
            value = value + up_part(last[-1], j)
        value = value * root_all + jnp.dot(mid, outmap_ref[:, lanes], preferred_element_type=F32)
        hid[c, j] = (value / (1.0 + jnp.exp(-value))).astype(BF16)
        for t2 in tens_to:
            hx_copy(t2, t, j).start()
        hp_copy(t, p, j).start()
        return carry

    lax.fori_loop(0, chunks, hidden_step, 0)

    def down_part(index, j):
        rows = pl.ds(pl.multiple_of(index * width + j * chunk, chunk), chunk)
        return jnp.dot(hid[index, j], w_down[rows, :], preferred_element_type=F32)

    down_copy(order[0]).wait()
    acc_down[...] = jnp.zeros_like(acc_down)

    def own_step(j, carry):
        acc_down[...] += down_part(c, j)
        return carry

    lax.fori_loop(0, chunks, own_step, 0)
    down_copy(order[1]).wait()

    def sibling_step(j, carry):
        hp_copy(t, q, j).wait_recv()
        acc_down[...] += down_part(t * 2 + q, j)
        return carry

    lax.fori_loop(0, chunks, sibling_step, 0)
    for t2 in tens_from:
        down_copy(t2 * 2 + p).wait()

        def across_step(j, carry, t2=t2):
            hx_copy(t2, t2, j).wait_recv()
            hp_copy(t2, p, j).start()
            acc_down[...] += down_part(t2 * 2 + p, j)
            return carry

        lax.fori_loop(0, chunks, across_step, 0)
    for t2 in tens_from:
        down_copy(t2 * 2 + q).wait()

        def diagonal_step(j, carry, t2=t2):
            hp_copy(t2, q, j).wait_recv()
            acc_down[...] += down_part(t2 * 2 + q, j)
            return carry

        lax.fori_loop(0, chunks, diagonal_step, 0)

    piece[...] = acc_down[...].astype(BF16)
    for z2 in node_to:
        go(remote(piece.at[at_block(z2)], ret.at[z], ret_s.at[z2], ret_r.at[z], {"node": z2}))

    def weight(node):
        expert = node // share
        return jnp.where(first_expert == expert, gate0, 0.0) + jnp.where(
            second_expert == expert, gate1, 0.0
        )

    mixed = head[...] + weight(z) * piece[at_block(z), :].astype(F32)
    for z2 in node_from:
        remote(ret.at[z2], ret.at[z2], ret_s.at[z2], ret_r.at[z2], {"node": z2}).wait_recv()
        mixed = mixed + weight(z2) * ret[z2].astype(F32)
    for index in range(groups):
        outb[index] = mixed[index * own : (index + 1) * own, :].astype(BF16)
    for c2 in chip_to:
        go(remote(outb.at[c2], out_ref.at[:, at_cols(c)], out_s.at[c2], out_r.at[c], to_chip(c2)))
    out_ref[:, at_cols(c)] = outb[c]
    for c2 in chip_from:
        remote(outb.at[c2], out_ref.at[:, at_cols(c2)], out_s.at[c2], out_r.at[c2], to_chip(c2)).wait_recv()

    for copy in sends:
        copy.wait_send()

    def drain(j, carry):
        for t2 in tens_to:
            hx_copy(t2, t, j).wait_send()
        hp_copy(t, p, j).wait_send()
        for t2 in tens_from:
            hp_copy(t2, p, j).wait_send()
        return carry

    lax.fori_loop(0, chunks, drain, 0)


def on_device(
    attention_partial,
    residual,
    norm_scale,
    router_matrix,
    up_matrix,
    down_matrix,
    adapter_in_maps,
    adapter_out_maps,
    token_experts,
    token_requests,
    request_adapters,
):
    nodes = lax.axis_size("node")
    tensors = lax.axis_size("tensor")
    groups = tensors * lax.axis_size("pair")
    share = nodes // EXPERT_COUNT
    own = residual.shape[2]
    block = attention_partial.shape[1]
    model = residual.shape[3]
    cols = model // groups
    width = up_matrix.shape[2]
    chunk = 512 if width % 512 == 0 else width
    chunks = width // chunk
    adapters, _, _, rank = adapter_in_maps.shape
    wide = adapters * rank
    tokens = nodes * block
    dims = (nodes, tensors, groups, own, block, cols, width, chunks, chunk, rank, adapters, share)
    in_columns = jnp.transpose(adapter_in_maps, (0, 1, 3, 2))
    vmem = pl.BlockSpec(memory_space=pltpu.VMEM)
    smem = pl.BlockSpec(memory_space=pltpu.SMEM)
    hbm = pl.BlockSpec(memory_space=pl.ANY)
    dma = pltpu.SemaphoreType.DMA
    mixed = pl.pallas_call(
        functools.partial(kernel, dims),
        out_shape=jax.ShapeDtypeStruct((own, model), BF16),
        in_specs=[hbm, vmem, vmem, vmem, hbm, hbm, hbm, vmem, smem, smem, smem],
        out_specs=vmem,
        scratch_shapes=[
            pltpu.VMEM((model, width), BF16),
            pltpu.VMEM((groups * width, cols), BF16),
            pltpu.VMEM((adapters, rank, cols), BF16),
            pltpu.VMEM((groups, block, cols), BF16),
            pltpu.VMEM((groups, own, cols), BF16),
            pltpu.VMEM((block, cols), F32),
            pltpu.VMEM((groups, tokens, cols), BF16),
            pltpu.VMEM((groups, 8, 128), jnp.int32),
            pltpu.VMEM((block, 128), jnp.int32),
            pltpu.VMEM((groups, block, 128), F32),
            pltpu.VMEM((nodes, block, 128), F32),
            pltpu.VMEM((groups, tokens, wide), BF16),
            pltpu.VMEM((chunks, tokens, chunk), F32),
            pltpu.VMEM((groups, chunks, tokens, chunk), BF16),
            pltpu.VMEM((tokens, cols), F32),
            pltpu.VMEM((tokens, cols), BF16),
            pltpu.VMEM((nodes, block, cols), BF16),
            pltpu.VMEM((groups, own, cols), BF16),
            dma((groups,)),
            dma((groups,)),
            dma((2,)),
            dma((groups,)),
            dma((groups,)),
            dma((groups,)),
            dma((groups,)),
            dma((groups,)),
            dma((groups,)),
            dma((groups,)),
            dma((groups,)),
            dma((nodes,)),
            dma((nodes,)),
            dma((nodes,)),
            dma((nodes,)),
            dma((tensors, nodes)),
            dma((tensors, nodes)),
            dma((tensors, nodes)),
            dma((tensors, nodes)),
            dma((groups,)),
            dma((groups,)),
            dma((tensors, chunks)),
            dma((tensors, chunks)),
            dma((tensors, chunks)),
            dma((tensors, chunks)),
            dma((nodes,)),
            dma((nodes,)),
            dma((groups,)),
            dma((groups,)),
        ],
        compiler_params=pltpu.CompilerParams(
            collective_id=0, has_side_effects=True, vmem_limit_bytes=60 * 1024 * 1024
        ),
        cost_estimate=pl.CostEstimate(
            flops=4 * tokens * model * width,
            bytes_accessed=4 * model * width,
            transcendentals=tokens * width,
        ),
    )(
        attention_partial[0],
        residual[0, 0],
        norm_scale[None, :],
        router_matrix.T,
        up_matrix[0],
        down_matrix[0],
        in_columns,
        adapter_out_maps.reshape(wide, width),
        token_experts[0, 0],
        token_requests[0, 0],
        request_adapters,
    )
    return mixed.reshape(1, 1, own, model)


def solution(mesh):
    in_specs = (
        P(("tensor", "pair"), ("groups", "node"), None),
        P(("groups", "node"), ("tensor", "pair"), None, None),
        P(),
        P(),
        P("node", None, ("tensor", "pair")),
        P("node", None, ("tensor", "pair")),
        P(None, None, ("tensor", "pair"), None),
        P(None, "node", None, ("tensor", "pair")),
        P(("groups", "node"), ("tensor", "pair"), None, None),
        P(("groups", "node"), ("tensor", "pair"), None),
        P("groups"),
    )
    out_specs = P(("groups", "node"), ("tensor", "pair"), None, None)
    return jax.shard_map(
        on_device, mesh=mesh, in_specs=in_specs, out_specs=out_specs, check_vma=False
    )
```

time: 134 us -> 46.1 us (0.34)
  Pallas kernels: 0 us -> 41.8 us
  waiting for transfers between devices: 36.7 us -> 0 us
  blocking collectives: 27.8 us -> 0 us
  matrix products: 24.4 us -> 0 us
  starting transfers between devices: 17.6 us -> 0 us
  between operations: 13.6 us -> 0.01 us
  other arithmetic: 6.83 us -> 0 us
  local copies, waits for them, and re-layouts: 6.43 us -> 4.1 us
    pallas_call x0 -> x1, Pallas kernels: none -> 41.8 us  [on_device(): pl.pallas_call(functools.partial(kernel, dims), out_shape=jax.ShapeDtypeS...]
    dot_general x7 -> x0, matrix products: 24.4 us -> none  [the longest x1 10.5 us: on_device(): jnp.dot(flat_rows, up_matrix[0], preferred_element_type=jnp.float32)]
    all_to_all x4 -> x0, waiting for transfers between devices: 21 us -> none  [the longest x1 6.75 us: on_device(): lax.all_to_all(arranged, 'node', split_axis=1, concat_axis=1, tiled=True)]
    all_gather x3 -> x0, blocking collectives: 21 us -> none  [the longest x1 7.91 us: on_device(): lax.all_gather(hidden, ('tensor', 'pair'), axis=1, tiled=True)]
    all_to_all x4 -> x0, starting transfers between devices: 17.6 us -> none  [the longest x1 6.32 us: on_device(): lax.all_to_all(send_ids, 'node', split_axis=0, concat_axis=0, tiled=True)]
    psum x1 -> x0, waiting for transfers between devices: 15 us -> none  [on_device(): lax.psum(partial_rows.astype(jnp.bfloat16), ('tensor', 'pair'))]
    psum x1 -> x0, blocking collectives: 6.84 us -> none  [on_device(): lax.psum(middle_part.astype(jnp.bfloat16), ('tensor', 'pair'))]
    reduce_sum x5 -> x0, other arithmetic: 2.3 us -> none  [the longest x1 1.09 us: on_device(): mean_square = jnp.mean(head_total * head_total, axis=1, keepdims=True)]
  transfers between devices with their start and end apart: 5 -> 0, of which waited for: 5 -> 0; matrix products, arithmetic and copies ran while one was open for 5% -> 0% of each run, Pallas kernels for 0% -> 0%
where the time goes in v1:
time: 46.1 us; the launch traced here: 45.9 us
  Pallas kernels  41.8 us (91%)
  local copies, waits for them, and re-layouts  4.1 us (9%)
    pallas_call x1, Pallas kernels, on_device(): pl.pallas_call(functools.partial(kernel, dims), out_shape=jax.ShapeDtypeS...  41.8 us
    unnamed x1, local copies, waits for them, and re-layouts  1.44 us
    squeeze x1, local copies, waits for them, and re-layouts, on_device(): token_experts[0, 0]  1.33 us
    broadcast_in_dim x1, local copies, waits for them, and re-layouts, on_device(): norm_scale[None, :]  1.33 us

profile of v1, /device:TPU:0, one launch (start us, length us, event | category | flops | bytes accessed | tf_op | source)
XLA Modules:
  0.0 45.9 jit_solution(3717614450250700781)
XLA Ops:
  0.0 1.3 %copy.12.te_ref = s32[4,2]{1,0:T(4,128)} copy(s32[4,2]{0,1:T(2,128)} %bitcast.18) | data formatting | bytes 64 | tf_op jit(solution)/shard_map/squeeze | solution.py:500
  1.3 1.3 %broadcast_in_dim.3.scale_ref = bf16[1,6144]{1,0:T(2,128)(2,1)} reshape(bf16[6144]{0:T(1024)(128)(2,1)} %param.13) | data formatting | bytes 24576 | tf_op jit(solution)/shard_map/broadcast_in_dim | solution.py:494
  2.7 41.8 %shard_map.109 = bf16[4,6144]{1,0:T(4,128)(2,1)} custom-call(bf16[16,6144]{1,0:T(8,128)(2,1)} %bitcast.14, bf16[4,6144]{1,0:T(4,128)(2,1)} %bitcast.16, bf16[1,6144]{1,0:T(2,128)(2,1)} %broadcast_in_dim.3.scale_ref, bf16[4,6144]{1,0:T(4,128)(2,1)} %bitcast.17, bf16[6144,2048]{1,0:T(8,128)(2,1)} %bitcast.10, bf16[8192,1536]{1,0:T(8,128)(2,1)} %bitcast.11, ...), custom_call_target="tpu_custom_call" | custom-call | flops 3221225472 | bytes 50331648 | tf_op jit(solution)/shard_map/pallas_call | solution.py:429
  44.4 1.4 %copy.14 = bf16[1,1,4,6144]{3,2,1,0:T(4,128)(2,1)} copy(bf16[1,1,4,6144]{3,2,1,0:T(4,128)(2,1)} %bitcast.15) | data formatting | bytes 98304

commit v2 on v1

--- a/solution.py
+++ b/solution.py
@@ -8,6 +8,7 @@
 from jax.sharding import PartitionSpec as P
 
 EXPERT_COUNT = 4
+CAP = 3
 MESH = pl.DeviceIdType.MESH
 F32 = jnp.float32
 BF16 = jnp.bfloat16
@@ -45,6 +46,7 @@
     piece,
     ret,
     outb,
+    scale_buf,
     up_sem,
     down_sem,
     loc_sem,
@@ -75,7 +77,7 @@
     out_s,
     out_r,
 ):
-    nodes, tensors, groups, own, block, cols, width, chunks, chunk, rank, adapters, share = dims
+    nodes, tensors, groups, own, block, cols, width, chunks, chunk, rank, adapters, share, cap = dims
     z = lax.axis_index("node")
     t = lax.axis_index("tensor")
     p = lax.axis_index("pair")
@@ -124,6 +126,12 @@
     for t2 in tens_from:
         order.append(t2 * 2 + q)
 
+    barrier = pltpu.get_barrier_semaphore()
+    for c2 in chip_to:
+        pl.semaphore_signal(barrier, inc=1, device_id=to_chip(c2), device_id_type=MESH)
+    for z2 in node_to:
+        pl.semaphore_signal(barrier, inc=1, device_id={"node": z2}, device_id_type=MESH)
+
     own_ap = pltpu.make_async_copy(ap_ref.at[:, at_cols(c)], ap_buf.at[c], loc_sem.at[0])
     own_ap.start()
     in_copy = pltpu.make_async_copy(in_ref.at[:, z // share], a_in, loc_sem.at[1])
@@ -131,20 +139,14 @@
     for index in order:
         up_copy(index).start()
 
-    barrier = pltpu.get_barrier_semaphore()
-    for c2 in chip_to:
-        pl.semaphore_signal(barrier, inc=1, device_id=to_chip(c2), device_id_type=MESH)
-    for z2 in node_to:
-        pl.semaphore_signal(barrier, inc=1, device_id={"node": z2}, device_id_type=MESH)
-
     row8 = lax.broadcasted_iota(jnp.int32, (8, 128), 0)
     lane8 = lax.broadcasted_iota(jnp.int32, (8, 128), 1)
     info = jnp.zeros((8, 128), jnp.int32)
     for k in range(own):
         here = row8 == k
         info = jnp.where(here & (lane8 == 0), ra_ref[tr_ref[k]], info)
-        info = jnp.where(here & (lane8 == 1), te_ref[k, 0], info)
-        info = jnp.where(here & (lane8 == 2), te_ref[k, 1], info)
+        info = jnp.where(here & (lane8 == 1), te_ref[0, k], info)
+        info = jnp.where(here & (lane8 == 2), te_ref[1, k], info)
     inf_buf[c] = info
 
     pl.semaphore_wait(barrier, groups - 1 + nodes - 1)
@@ -157,6 +159,7 @@
         go(remote(inf_buf.at[c], inf_buf.at[c], inf_s.at[c2], inf_r.at[c], to_chip(c2)))
 
     res_buf[c] = res_ref[:, at_cols(c)]
+    scale_buf[...] = scale_ref[...].astype(F32).reshape(1, groups * cols)
     for c2 in chip_from:
         remote(res_buf.at[c2], res_buf.at[c2], res_s.at[c2], res_r.at[c2], to_chip(c2)).wait_recv()
     for index in range(groups):
@@ -169,7 +172,7 @@
         total = total + ap_buf[index].astype(F32)
     total = total + head[...]
     head[...] = total
-    scale = scale_ref[:, at_cols(c)].astype(F32)
+    scale = scale_buf[:, at_cols(c)]
     y = (total * scale).astype(BF16)
     y_buf[c, at_block(z), :] = y
 
@@ -206,6 +209,20 @@
         go(remote(part_buf.at[c], part_buf.at[c], part_s.at[c2], part_r.at[c], to_chip(c2)))
     for index in order:
         down_copy(index).start()
+    for z2 in node_from:
+        z_copy(z2, z2).wait_recv()
+        spread(z2)
+
+    in_copy.wait()
+    wide = adapters * rank
+    mid = lax.dot_general(
+        y_buf[c], a_in[...].reshape(wide, cols), (((1,), (1,)), ((), ())),
+        preferred_element_type=F32,
+    )
+    lora_buf[c] = mid.astype(BF16)
+    for c2 in chip_to:
+        go(remote(lora_buf.at[c], lora_buf.at[c], lora_s.at[c2], lora_r.at[c], to_chip(c2)))
+
     for c2 in chip_from:
         remote(inf_buf.at[c2], inf_buf.at[c2], inf_s.at[c2], inf_r.at[c2], to_chip(c2)).wait_recv()
     for index in range(groups):
@@ -218,7 +235,13 @@
     root = lax.rsqrt(sums[:, 0:1] / (groups * cols) + 1e-05)
     routes = inf_all[...]
     meta[z] = jnp.where(
-        lane == 0, root, jnp.where(lane == 1, routes[:, 0:1].astype(F32), 0.0)
+        lane == 0,
+        root,
+        jnp.where(
+            lane == 1,
+            routes[:, 0:1].astype(F32),
+            jnp.where(lane == 2, routes[:, 1:2], routes[:, 2:3]).astype(F32),
+        ),
     )
     for z2 in node_to:
         go(remote(meta.at[z], meta.at[z], meta_s.at[z2], meta_r.at[z], {"node": z2}))
@@ -233,20 +256,6 @@
     gate0 = 1.0 / (1.0 + jnp.exp(chosen1 - chosen0))
     gate1 = 1.0 - gate0
 
-    for z2 in node_from:
-        z_copy(z2, z2).wait_recv()
-        spread(z2)
-
-    in_copy.wait()
-    wide = adapters * rank
-    mid = lax.dot_general(
-        y_buf[c], a_in[...].reshape(wide, cols), (((1,), (1,)), ((), ())),
-        preferred_element_type=F32,
-    )
-    lora_buf[c] = mid.astype(BF16)
-    for c2 in chip_to:
-        go(remote(lora_buf.at[c], lora_buf.at[c], lora_s.at[c2], lora_r.at[c], to_chip(c2)))
-
     def up_part(index, j):
         lanes = pl.ds(pl.multiple_of(j * chunk, chunk), chunk)
         rows = at_cols(index)
@@ -285,6 +294,21 @@
     slot = lax.broadcasted_iota(jnp.int32, (tokens, wide), 1).astype(F32)
     mid = jnp.where((slot >= low) & (slot < low + rank), mid * root_all, 0.0).astype(BF16)
 
+    expert_here = (z // share).astype(F32)
+    routed = jnp.where(
+        (facts[:, 2:3] == expert_here) | (facts[:, 3:4] == expert_here), 1.0, 0.0
+    )
+    below = lax.broadcasted_iota(jnp.int32, (tokens, tokens), 0) > lax.broadcasted_iota(
+        jnp.int32, (tokens, tokens), 1
+    )
+    place = jnp.dot(
+        below.astype(F32).astype(BF16),
+        jnp.broadcast_to(routed, (tokens, 128)).astype(BF16),
+        preferred_element_type=F32,
+    )[:, 0:1]
+    slots = lax.broadcasted_iota(jnp.int32, (tokens, cap), 1).astype(F32)
+    pack = jnp.where((routed > 0.0) & (slots == place), 1.0, 0.0).astype(BF16)
+
     last = [t2 * 2 + q for t2 in tens_from]
     for i, t2 in enumerate(tens_from):
         for zb in range(nodes):
@@ -309,7 +333,10 @@
         if last:
             value = value + up_part(last[-1], j)
         value = value * root_all + jnp.dot(mid, outmap_ref[:, lanes], preferred_element_type=F32)
-        hid[c, j] = (value / (1.0 + jnp.exp(-value))).astype(BF16)
+        value = (value / (1.0 + jnp.exp(-value))).astype(BF16)
+        hid[c, j] = lax.dot_general(
+            pack, value, (((0,), (0,)), ((), ())), preferred_element_type=F32
+        ).astype(BF16)
         for t2 in tens_to:
             hx_copy(t2, t, j).start()
         hp_copy(t, p, j).start()
@@ -357,7 +384,9 @@
 
         lax.fori_loop(0, chunks, diagonal_step, 0)
 
-    piece[...] = acc_down[...].astype(BF16)
+    piece[...] = jnp.dot(
+        pack, acc_down[...].astype(BF16), preferred_element_type=F32
+    ).astype(BF16)
     for z2 in node_to:
         go(remote(piece.at[at_block(z2)], ret.at[z], ret_s.at[z2], ret_r.at[z], {"node": z2}))
 
@@ -420,7 +449,8 @@
     adapters, _, _, rank = adapter_in_maps.shape
     wide = adapters * rank
     tokens = nodes * block
-    dims = (nodes, tensors, groups, own, block, cols, width, chunks, chunk, rank, adapters, share)
+    cap = tokens // own * CAP
+    dims = (nodes, tensors, groups, own, block, cols, width, chunks, chunk, rank, adapters, share, cap)
     in_columns = jnp.transpose(adapter_in_maps, (0, 1, 3, 2))
     vmem = pl.BlockSpec(memory_space=pltpu.VMEM)
     smem = pl.BlockSpec(memory_space=pltpu.SMEM)
@@ -445,11 +475,12 @@
             pltpu.VMEM((nodes, block, 128), F32),
             pltpu.VMEM((groups, tokens, wide), BF16),
             pltpu.VMEM((chunks, tokens, chunk), F32),
-            pltpu.VMEM((groups, chunks, tokens, chunk), BF16),
-            pltpu.VMEM((tokens, cols), F32),
+            pltpu.VMEM((groups, chunks, cap, chunk), BF16),
+            pltpu.VMEM((cap, cols), F32),
             pltpu.VMEM((tokens, cols), BF16),
             pltpu.VMEM((nodes, block, cols), BF16),
             pltpu.VMEM((groups, own, cols), BF16),
+            pltpu.VMEM((1, model), F32),
             dma((groups,)),
             dma((groups,)),
             dma((2,)),
@@ -491,13 +522,13 @@
     )(
         attention_partial[0],
         residual[0, 0],
-        norm_scale[None, :],
+        norm_scale,
         router_matrix.T,
         up_matrix[0],
         down_matrix[0],
         in_columns,
         adapter_out_maps.reshape(wide, width),
-        token_experts[0, 0],
+        token_experts[0, 0].T,
         token_requests[0, 0],
         request_adapters,
     )

time: 46.1 us -> 42.7 us (0.926)
  local copies, waits for them, and re-layouts: 4.1 us -> 1.44 us
  Pallas kernels: 41.8 us -> 41.1 us
    squeeze x1 -> x0, local copies, waits for them, and re-layouts: 1.33 us -> none  [on_device(): token_experts[0, 0]]
    broadcast_in_dim x1 -> x0, local copies, waits for them, and re-layouts: 1.33 us -> none  [on_device(): norm_scale[None, :]]
    pallas_call x1, Pallas kernels: 41.8 us -> 41.1 us  [on_device(): pl.pallas_call(functools.partial(kernel, dims), out_shape=jax.ShapeDtypeS...]
where the time goes in v2:
time: 42.7 us; the launch traced here: 42.5 us
  Pallas kernels  41.1 us (96%)
  local copies, waits for them, and re-layouts  1.44 us (3%)
    pallas_call x1, Pallas kernels, on_device(): pl.pallas_call(functools.partial(kernel, dims), out_shape=jax.ShapeDtypeS...  41.1 us
    unnamed x1, local copies, waits for them, and re-layouts  1.44 us

profile of v2, /device:TPU:0, one launch (start us, length us, event | category | flops | bytes accessed | tf_op | source)
XLA Modules:
  0.0 42.5 jit_solution(14475229973951057869)
XLA Ops:
  0.0 41.1 %shard_map.109 = bf16[4,6144]{1,0:T(4,128)(2,1)} custom-call(bf16[16,6144]{1,0:T(8,128)(2,1)} %bitcast.16, bf16[4,6144]{1,0:T(4,128)(2,1)} %bitcast.18, bf16[6144]{0:T(1024)(128)(2,1)} %scale_ref.1, bf16[4,6144]{1,0:T(4,128)(2,1)} %bitcast.19, bf16[6144,2048]{1,0:T(8,128)(2,1)} %bitcast.12, bf16[8192,1536]{1,0:T(8,128)(2,1)} %bitcast.13, ...), custom_call_target="tpu_custom_call" | custom-call | flops 3221225472 | bytes 50331648 | tf_op jit(solution)/shard_map/pallas_call | solution.py:459
  41.1 1.4 %copy.13 = bf16[1,1,4,6144]{3,2,1,0:T(4,128)(2,1)} copy(bf16[1,1,4,6144]{3,2,1,0:T(4,128)(2,1)} %bitcast.17) | data formatting | bytes 98304

commit v3 on v2

--- a/solution.py
+++ b/solution.py
@@ -444,7 +444,7 @@
     model = residual.shape[3]
     cols = model // groups
     width = up_matrix.shape[2]
-    chunk = 512 if width % 512 == 0 else width
+    chunk = 1024 if width % 1024 == 0 else width
     chunks = width // chunk
     adapters, _, _, rank = adapter_in_maps.shape
     wide = adapters * rank

time: 42.7 us -> 41.9 us (0.981)
  Pallas kernels: 41.1 us -> 40.3 us
    pallas_call x1, Pallas kernels: 41.1 us -> 40.3 us  [on_device(): pl.pallas_call(functools.partial(kernel, dims), out_shape=jax.ShapeDtypeS...]
where the time goes in v3:
time: 41.9 us; the launch traced here: 41.7 us
  Pallas kernels  40.3 us (96%)
  local copies, waits for them, and re-layouts  1.44 us (3%)
    pallas_call x1, Pallas kernels, on_device(): pl.pallas_call(functools.partial(kernel, dims), out_shape=jax.ShapeDtypeS...  40.3 us
    unnamed x1, local copies, waits for them, and re-layouts  1.44 us

profile of v3, /device:TPU:0, one launch (start us, length us, event | category | flops | bytes accessed | tf_op | source)
XLA Modules:
  0.0 41.7 jit_solution(2977572182209043519)
XLA Ops:
  0.0 40.3 %shard_map.109 = bf16[4,6144]{1,0:T(4,128)(2,1)} custom-call(bf16[16,6144]{1,0:T(8,128)(2,1)} %bitcast.16, bf16[4,6144]{1,0:T(4,128)(2,1)} %bitcast.18, bf16[6144]{0:T(1024)(128)(2,1)} %scale_ref.1, bf16[4,6144]{1,0:T(4,128)(2,1)} %bitcast.19, bf16[6144,2048]{1,0:T(8,128)(2,1)} %bitcast.12, bf16[8192,1536]{1,0:T(8,128)(2,1)} %bitcast.13, ...), custom_call_target="tpu_custom_call" | custom-call | flops 3221225472 | bytes 50331648 | tf_op jit(solution)/shard_map/pallas_call | solution.py:459
  40.3 1.4 %copy.13 = bf16[1,1,4,6144]{3,2,1,0:T(4,128)(2,1)} copy(bf16[1,1,4,6144]{3,2,1,0:T(4,128)(2,1)} %bitcast.17) | data formatting | bytes 98304
